TPU v7x, 32 devices: a whole 2x2x4 slice. The times are simulated.
32 devices in a mesh: grp: 2 (over x), row: 8 (over z, y), col: 2 (over core).
Axes of the slice: x: 2, y: 2, z: 4, core: 2. Of those that a mesh axis runs over, the one named last changes fastest.
Arguments:
- green: float32 [4, 256, 256, 256], P('grp', None, 'row', 'col'), parts along dimension 0, may hold values from -6 to 6
- hamiltonian: float32 [4, 256, 256], P('grp'), parts along dimension 0
- onebody: float32 [4, 256, 256], P('grp'), parts along dimension 0, may hold values from -5 to 5
- site_map: int32 [256], replicated, may hold values from 0 to 31
- onsite_u: float32 [32], replicated, may hold values from 0.5 to 2
- pair_first: int32 [4096], replicated, may hold values from 0 to 255
- pair_second: int32 [4096], replicated, may hold values from 0 to 255
Outputs:
- advanced: float32 [4, 256, 256, 256], P('grp', None, 'row', 'col'), parts along dimension 0
There are 2 independent parts, one for each index of `grp`. A program takes and returns all parts, laid end to end along the dimension named above; an argument that names none is the same for every part. Nothing has to cross between parts.
All inputs are finite; a program needn't handle non-finite values.
Results may differ from a plain program's by a relative error of at most 0.00005.
Values sent between devices are 32-bit elements; how exact they have to be, the bound alone decides.
A program may use at most 192 MiB of HBM per device.

v0:
```python
import jax
import jax.numpy as jnp
from jax import lax
from jax.sharding import PartitionSpec as P

time_step = 0.1
highest = lax.Precision.HIGHEST


def along_rows(hamiltonian, field):
    hre = hamiltonian[0]
    him = hamiltonian[1]
    out_re = jnp.einsum("ia,kaj->kij", hre, field[0], precision=highest) - jnp.einsum(
        "ia,kaj->kij", him, field[1], precision=highest
    )
    out_im = jnp.einsum("ia,kaj->kij", hre, field[1], precision=highest) + jnp.einsum(
        "ia,kaj->kij", him, field[0], precision=highest
    )
    return jnp.stack([out_re, out_im])


def along_cols(hamiltonian, field):
    hre = hamiltonian[0]
    him = hamiltonian[1]
    out_re = jnp.einsum("ja,kia->kij", hre, field[0], precision=highest) - jnp.einsum(
        "ja,kia->kij", him, field[1], precision=highest
    )
    out_im = jnp.einsum("ja,kia->kij", hre, field[1], precision=highest) + jnp.einsum(
        "ja,kia->kij", him, field[0], precision=highest
    )
    return jnp.stack([out_re, out_im])


def on_device(green, hamiltonian, onebody, site_map, onsite_u, pair_first, pair_second):
    orbs = green.shape[1]
    nrows = green.shape[2]
    ncols = green.shape[3]
    row_start = lax.axis_index("row") * nrows
    col_start = lax.axis_index("col") * ncols
    sites_i = lax.dynamic_slice_in_dim(site_map, row_start, nrows)
    sites_j = lax.dynamic_slice_in_dim(site_map, col_start, ncols)
    levels = jnp.arange(onsite_u.shape[0], dtype=jnp.int32)
    u_rows = jnp.sum(jnp.where(sites_i[:, None] == levels[None, :], onsite_u[None, :], 0.0), axis=1)
    ladder = u_rows[:, None] * (sites_i[:, None] == sites_j[None, :]).astype(jnp.float32)
    first_hot = (
        pair_first[:, None] == (row_start + jnp.arange(nrows, dtype=jnp.int32))[None, :]
    ).astype(jnp.float32)
    second_hot = (
        pair_second[:, None] == (col_start + jnp.arange(ncols, dtype=jnp.int32))[None, :]
    ).astype(jnp.float32)
    counts = jnp.einsum("pi,pj->ij", first_hot, second_hot, precision=highest)
    pauli = u_rows[:, None] * counts
    left = lax.dynamic_slice_in_dim(onebody, row_start, nrows, 2)
    right = lax.dynamic_slice_in_dim(onebody, col_start, ncols, 2)
    source_re = pauli * (
        left[0][:, :, None] * right[0][:, None, :] - left[1][:, :, None] * right[1][:, None, :]
    )
    source_im = pauli * (
        left[0][:, :, None] * right[1][:, None, :] + left[1][:, :, None] * right[0][:, None, :]
    )
    hre = hamiltonian[0]
    him = hamiltonian[1]

    def row_apply(field):
        return along_rows(hamiltonian, field)

    def col_apply(field):
        return along_cols(hamiltonian, field)

    def force(field):
        flat_re = field[0].reshape(orbs, nrows * ncols)
        flat_im = field[1].reshape(orbs, nrows * ncols)
        k_re = (
            jnp.dot(hre, flat_re, precision=highest) - jnp.dot(him, flat_im, precision=highest)
        ).reshape(orbs, nrows, ncols)
        k_im = (
            jnp.dot(hre, flat_im, precision=highest) + jnp.dot(him, flat_re, precision=highest)
        ).reshape(orbs, nrows, ncols)
        moved_rows = row_apply(
            lax.all_to_all(field, "row", split_axis=1, concat_axis=2, tiled=True)
        )
        by_rows = lax.all_to_all(moved_rows, "row", split_axis=2, concat_axis=1, tiled=True)
        moved_cols = col_apply(
            lax.all_to_all(field, "col", split_axis=1, concat_axis=3, tiled=True)
        )
        by_cols = lax.all_to_all(moved_cols, "col", split_axis=3, concat_axis=1, tiled=True)
        cross = by_rows + by_cols
        total_re = k_re + cross[0] + ladder * field[0] + source_re
        total_im = k_im + cross[1] + ladder * field[1] + source_im
        return jnp.stack([total_im, -total_re])

    half = green + 0.5 * time_step * force(green)
    return green + time_step * force(half)


def solution(mesh):
    placed = (
        P("grp", None, "row", "col"),
        P("grp", None, None),
        P("grp", None, None),
        P(),
        P(),
        P(),
        P(),
    )
    return jax.shard_map(
        on_device,
        mesh=mesh,
        in_specs=placed,
        out_specs=P("grp", None, "row", "col"),
        check_vma=False,
    )
```

profile of v0, /device:TPU:0, one launch (start us, length us, event | category | flops | bytes accessed | tf_op | source)
XLA Modules:
  0.0 991.6 jit_solution(16488565198921307543)
XLA Ops:
  7.8 11.8 %all_to_all.132 = f32[2,256,32,128]{3,2,0,1:T(8,128)} all-to-all(f32[2,256,32,128]{3,2,0,1:T(8,128)S(1)} %copy.88), channel_id=1, replica_groups=mesh['grp'=2,'row'=8,'col'=2] {'col'}, dimensions={1} | all-to-all | bytes 16777216 | tf_op jit(solution)/shard_map/all_to_all | solution.py:84
  19.6 7.3 all-to-all-start
  26.9 15.3 %copy.175 = f32[2,2,128,32,128]{4,1,2,3,0:T(2,128)} copy(f32[2,2,128,32,128]{4,3,0,2,1:T(8,128)} %bitcast.225) | data formatting | bytes 16777216 | tf_op jit(solution)/shard_map/all_to_all | solution.py:84
  42.2 7.8 fusion.107
  83.1 10.3 %copy.101 = f32[2,128,32,256]{1,2,0,3:T(8,128)} copy(f32[2,128,32,256]{3,1,2,0:T(8,128)} %pad_maximum_fusion.1) | data formatting | bytes 16777216 | tf_op jit(solution)/shard_map/stack | solution.py:31
  93.4 117.0 %all-to-all-done = f32[2,256,32,128]{3,2,0,1:T(8,128)} async-done(((f32[2,256,32,128]{3,2,0,1:T(8,128)}), f32[2,256,32,128]{3,2,0,1:T(8,128)}, u32[]{:S(2)}, u32[]{:S(2)}) %all-to-all-start) | async-done | bytes 8388640 | tf_op jit(solution)/shard_map/all_to_all | solution.py:80
  210.3 7.4 all-to-all-start.3
  245.1 7.3 add_bitcast_fusion.3
  256.4 10.3 %copy.96 = f32[2,32,256,128]{3,1,0,2:T(8,128)} copy(f32[2,32,256,128]{2,3,1,0:T(8,128)} %pad_maximum_fusion) | data formatting | bytes 16777216 | tf_op jit(solution)/shard_map/stack | solution.py:19
  272.0 11.3 %copy.102 = f32[2,128,32,2,128]{4,2,1,3,0:T(8,128)} copy(f32[2,128,32,2,128]{1,2,0,4,3:T(8,128)} %bitcast.21) | data formatting | bytes 16777216 | tf_op jit(solution)/shard_map/all_to_all | solution.py:86
  318.6 137.2 %all-to-all-done.1 = f32[2,32,256,128]{3,1,0,2:T(8,128)} async-done(((f32[2,32,256,128]{3,1,0,2:T(8,128)}), f32[2,32,256,128]{3,1,0,2:T(8,128)}, u32[]{:S(2)}, u32[]{:S(2)}) %all-to-all-start.1) | async-done | bytes 8388640 | tf_op jit(solution)/shard_map/all_to_all | solution.py:82
  455.8 13.3 %copy.98 = f32[2,8,32,32,128]{4,3,2,1,0:T(8,128)} copy(f32[2,8,32,32,128]{4,2,0,3,1:T(8,128)} %bitcast.15) | data formatting | bytes 16777216 | tf_op jit(solution)/shard_map/all_to_all | solution.py:82
  469.1 11.8 %add.130 = f32[2,256,32,128]{3,2,1,0:T(8,128)} add(f32[2,256,32,128]{3,2,1,0:T(8,128)} %bitcast.223, f32[2,256,32,128]{3,2,1,0:T(8,128)} %bitcast.221) | non-fusion elementwise | flops 2097152 | bytes 25165824 | tf_op jit(solution)/shard_map/add | solution.py:87
  480.9 13.6 %fusion.12 = (f32[1,256,32,128]{3,2,1,0:T(8,128)S(1)}, f32[1,256,32,128]{3,2,1,0:T(8,128)}) fusion(f32[2,256,32,128]{3,2,1,0:T(8,128)} %add.130, f32[256,128]{1,0:T(8,128)S(1)} %get-tuple-element.24, f32[256,32]{1,0:T(8,128)S(1)} %get-tuple-element.22, f32[256,128]{1,0:T(8,128)S(1)} %get-tuple-element.23, f32[256,32]{1,0:T(8,128)S(1)} %get-tuple-element.21, ...), kind=kLoop, calls=%fused_computation.26 | loop fusion | flops 17825792 | bytes 33914880 | tf_op jit(solution)/shard_map/add | solution.py:89
  505.5 11.8 %all_to_all.133 = f32[2,256,32,128]{3,2,0,1:T(8,128)} all-to-all(f32[2,256,32,128]{3,2,0,1:T(8,128)S(1)} %copy.103), channel_id=1, replica_groups=mesh['grp'=2,'row'=8,'col'=2] {'col'}, dimensions={1} | all-to-all | bytes 16777216 | tf_op jit(solution)/shard_map/all_to_all | solution.py:84
  522.3 15.4 %copy.174 = f32[2,2,128,32,128]{4,1,2,3,0:T(2,128)} copy(f32[2,2,128,32,128]{4,3,0,2,1:T(8,128)} %bitcast.226) | data formatting | bytes 16777216 | tf_op jit(solution)/shard_map/all_to_all | solution.py:84
  537.7 7.7 fusion.104
  578.5 10.3 %copy.116 = f32[2,128,32,256]{1,2,0,3:T(8,128)} copy(f32[2,128,32,256]{3,1,2,0:T(8,128)} %pad_maximum_fusion.3) | data formatting | bytes 16777216 | tf_op jit(solution)/shard_map/stack | solution.py:31
  588.8 117.1 %all-to-all-done.4 = f32[2,256,32,128]{3,2,0,1:T(8,128)} async-done(((f32[2,256,32,128]{3,2,0,1:T(8,128)}), f32[2,256,32,128]{3,2,0,1:T(8,128)}, u32[]{:S(2)}, u32[]{:S(2)}) %all-to-all-start.4) | async-done | bytes 8388640 | tf_op jit(solution)/shard_map/all_to_all | solution.py:80
  705.9 7.4 all-to-all-start.7
  733.6 7.1 subtract_bitcast_fusion.1
  740.8 7.3 add_bitcast_fusion.1
  751.9 10.3 %copy.111 = f32[2,32,256,128]{3,1,0,2:T(8,128)} copy(f32[2,32,256,128]{2,3,1,0:T(8,128)} %pad_maximum_fusion.2) | data formatting | bytes 16777216 | tf_op jit(solution)/shard_map/stack | solution.py:19
  767.6 10.9 %copy.117 = f32[2,128,32,2,128]{4,2,1,3,0:T(8,128)} copy(f32[2,128,32,2,128]{1,2,0,4,3:T(8,128)} %bitcast.47) | data formatting | bytes 16777216 | tf_op jit(solution)/shard_map/all_to_all | solution.py:86
  783.0 8.4 fusion.6
  791.4 11.8 %convolution_add_fusion = f32[4096,256]{1,0:T(8,128)} fusion(f32[4096,256]{1,0:T(8,128)S(1)} %fusion.6, f32[32,8,32,128]{3,2,1,0:T(8,128)S(1)} %bitcast.207, f32[2,256,256]{2,1,0:T(8,128)S(1)} %copy-done.1), kind=kOutput, calls=%fused_computation.11 | convolution fusion | flops 3222274048 | bytes 12845056 | tf_op jit(solution)/shard_map/dot_general | solution.py:77
  808.7 9.8 fusion.2
  818.5 11.6 %convolution_subtract_fusion = f32[4096,256]{1,0:T(8,128)} fusion(f32[4096,256]{1,0:T(8,128)S(1)} %fusion.2, f32[32,8,32,128]{3,2,1,0:T(8,128)S(1)} %bitcast.206, f32[2,256,256]{2,1,0:T(8,128)S(1)} %copy-done.1), kind=kOutput, calls=%fused_computation.10 | convolution fusion | flops 3222274048 | bytes 12845056 | tf_op jit(solution)/shard_map/dot_general | solution.py:74
  835.8 115.7 %all-to-all-done.5 = f32[2,32,256,128]{3,1,0,2:T(8,128)} async-done(((f32[2,32,256,128]{3,1,0,2:T(8,128)}), f32[2,32,256,128]{3,1,0,2:T(8,128)}, u32[]{:S(2)}, u32[]{:S(2)}) %all-to-all-start.5) | async-done | bytes 8388640 | tf_op jit(solution)/shard_map/all_to_all | solution.py:82
  951.6 13.1 %copy.113 = f32[2,8,32,32,128]{4,3,2,1,0:T(8,128)} copy(f32[2,8,32,32,128]{4,2,0,3,1:T(8,128)} %bitcast.41) | data formatting | bytes 16777216 | tf_op jit(solution)/shard_map/all_to_all | solution.py:82
  964.7 11.3 %add.150 = f32[2,256,32,128]{3,2,1,0:T(8,128)} add(f32[2,256,32,128]{3,2,1,0:T(8,128)} %bitcast.224, f32[2,256,32,128]{3,2,1,0:T(8,128)} %bitcast.222) | non-fusion elementwise | flops 2097152 | bytes 25165824 | tf_op jit(solution)/shard_map/add | solution.py:87
  976.0 10.9 %fusion.23 = (f32[1,256,32,128]{3,2,1,0:T(8,128)S(1)}, f32[1,256,32,128]{3,2,1,0:T(8,128)S(1)}) fusion(f32[1,256,32,128]{3,2,1,0:T(8,128)} %copy.118, f32[2,256,32,128]{3,2,1,0:T(8,128)} %add.150, f32[256,128]{1,0:T(8,128)S(1)} %get-tuple-element.24, f32[256,32]{1,0:T(8,128)S(1)} %get-tuple-element.22, f32[256,128]{1,0:T(8,128)S(1)} %get-tuple-element.23, ...), kind=kLoop, calls=%fused_computation.39 | loop fusion | flops 17825792 | bytes 33914880 | tf_op jit(solution)/shard_map/add | solution.py:89
  (101 shorter events, 210.9 us)
Async XLA Ops:
  4.4 3.4 copy-start.2
  19.6 190.7 %all-to-all-start = ((f32[2,256,32,128]{3,2,0,1:T(8,128)}), f32[2,256,32,128]{3,2,0,1:T(8,128)}, u32[]{:S(2)}, u32[]{:S(2)}) async-start(f32[2,256,32,128]{3,2,0,1:T(8,128)} %copy-done.2), calls=%async_computation | async-start | bytes 16777216 | tf_op jit(solution)/shard_map/all_to_all | solution.py:80
  56.5 6.5 copy-start.1
  63.0 5.6 copy-start.7
  72.2 3.5 copy-start.9
  210.3 56.4 %all-to-all-start.3 = ((f32[2,128,32,256]{1,2,0,3:T(8,128)}), f32[2,128,32,256]{1,2,0,3:T(8,128)}, u32[]{:S(2)}, u32[]{:S(2)}) async-start(f32[2,128,32,256]{1,2,0,3:T(8,128)} %copy.101), calls=%async_computation.3 | async-start | bytes 16777216 | tf_op jit(solution)/shard_map/all_to_all | solution.py:86
  266.7 5.1 copy-start.15
  266.7 189.1 %all-to-all-start.1 = ((f32[2,32,256,128]{3,1,0,2:T(8,128)}), f32[2,32,256,128]{3,1,0,2:T(8,128)}, u32[]{:S(2)}, u32[]{:S(2)}) async-start(f32[2,32,256,128]{3,1,0,2:T(8,128)} %copy.96), calls=%async_computation.1 | async-start | bytes 16777216 | tf_op jit(solution)/shard_map/all_to_all | solution.py:82
  314.6 2.8 copy-start.16
  314.6 2.9 copy-start.12
  314.7 3.2 copy-start.13
  314.7 3.2 copy-start.14
  469.1 11.8 %copy-start.11 = (f32[32,8,32,128]{3,2,1,0:T(8,128)S(1)}, f32[32,8,32,128]{3,2,1,0:T(8,128)}, u32[]{:S(2)}) copy-start(f32[32,8,32,128]{3,2,1,0:T(8,128)} %copy.132) | copy-start | bytes 12582916
  480.9 13.6 %slice-start = ((s8[8388608]{0:T(1024)(128)(4,1)}), s8[4194304]{0:T(1024)(128)(4,1)S(1)}, s32[]{:S(2)}) async-start(s8[8388608]{0:T(1024)(128)(4,1)} %bitcast.201), calls=%async_computation.8 | async-start | bytes 8388608
  480.9 13.6 %slice-start.1 = ((s8[8388608]{0:T(1024)(128)(4,1)}), s8[4194304]{0:T(1024)(128)(4,1)S(1)}, s32[]{:S(2)}) async-start(s8[8388608]{0:T(1024)(128)(4,1)} %bitcast.201), calls=%async_computation.9 | async-start | bytes 8388608
  498.2 4.0 copy-start
  502.3 3.3 copy-start.3
  517.3 188.6 %all-to-all-start.4 = ((f32[2,256,32,128]{3,2,0,1:T(8,128)}), f32[2,256,32,128]{3,2,0,1:T(8,128)}, u32[]{:S(2)}, u32[]{:S(2)}) async-start(f32[2,256,32,128]{3,2,0,1:T(8,128)} %copy-done.3), calls=%async_computation.4 | async-start | bytes 16777216 | tf_op jit(solution)/shard_map/all_to_all | solution.py:80
  558.4 5.6 copy-start.8
  567.6 3.5 copy-start.10
  705.9 56.3 %all-to-all-start.7 = ((f32[2,128,32,256]{1,2,0,3:T(8,128)}), f32[2,128,32,256]{1,2,0,3:T(8,128)}, u32[]{:S(2)}, u32[]{:S(2)}) async-start(f32[2,128,32,256]{1,2,0,3:T(8,128)} %copy.116), calls=%async_computation.7 | async-start | bytes 16777216 | tf_op jit(solution)/shard_map/all_to_all | solution.py:86
  762.2 189.3 %all-to-all-start.5 = ((f32[2,32,256,128]{3,1,0,2:T(8,128)}), f32[2,32,256,128]{3,1,0,2:T(8,128)}, u32[]{:S(2)}, u32[]{:S(2)}) async-start(f32[2,32,256,128]{3,1,0,2:T(8,128)} %copy.111), calls=%async_computation.5 | async-start | bytes 16777216 | tf_op jit(solution)/shard_map/all_to_all | solution.py:82
  782.9 8.4 copy-start.4
  783.0 8.4 copy-start.6
  808.7 9.8 copy-start.5
  964.7 22.3 %slice-start.2 = ((s8[8388608]{0:T(1024)(128)(4,1)}), s8[4194304]{0:T(1024)(128)(4,1)S(1)}, s32[]{:S(2)}) async-start(s8[8388608]{0:T(1024)(128)(4,1)} %bitcast.203), calls=%async_computation.10 | async-start | bytes 8388608
  976.0 10.9 %slice-start.3 = ((s8[8388608]{0:T(1024)(128)(4,1)}), s8[4194304]{0:T(1024)(128)(4,1)S(1)}, s32[]{:S(2)}) async-start(s8[8388608]{0:T(1024)(128)(4,1)} %bitcast.203), calls=%async_computation.11 | async-start | bytes 8388608
where the time goes:
time: 1000 us; the launch traced here: 992 us
  waiting for transfers between devices  487 us (49%)
  local copies, waits for them, and re-layouts  216 us (22%)
  matrix products  155 us (16%)
  other arithmetic  71.4 us (7%)
  starting transfers between devices  37.5 us (4%)
  blocking collectives  23.6 us (2%)
    all_to_all x2, waiting for transfers between devices, force(): lax.all_to_all(moved_rows, 'row', split_axis=2, concat_axis=1, tiled=True)  253 us
    all_to_all x2, waiting for transfers between devices, force(): lax.all_to_all(field, 'row', split_axis=1, concat_axis=2, tiled=True)  234 us
    all_to_all x2, local copies, waits for them, and re-layouts, force(): lax.all_to_all(field, 'col', split_axis=1, concat_axis=3, tiled=True)  30.8 us
    all_to_all x2, local copies, waits for them, and re-layouts, force(): lax.all_to_all(moved_rows, 'row', split_axis=2, concat_axis=1, tiled=True)  26.4 us
    add x2, other arithmetic, force(): total_im = k_im + cross[1] + ladder * field[1] + source_im  24.5 us
    all_to_all x2, blocking collectives, force(): lax.all_to_all(field, 'col', split_axis=1, concat_axis=3, tiled=True)  23.6 us
    add x2, other arithmetic, force(): cross = by_rows + by_cols  23.2 us
    all_to_all x2, local copies, waits for them, and re-layouts, force(): lax.all_to_all(moved_cols, 'col', split_axis=3, concat_axis=1, tiled=True)  22.2 us
  transfers between devices with their start and end apart: 6, of which 4 were waited for; matrix products, arithmetic and copies ran while one was open for 35% of the time, Pallas kernels for 0%

commit v1 on v0

v1 whole, which is shorter than its diff:
```python
import functools

import jax
import jax.numpy as jnp
from jax import lax
from jax.experimental import pallas as pl
from jax.experimental.pallas import tpu as pltpu
from jax.sharding import Mesh, PartitionSpec as P

time_step = 0.1
highest = lax.Precision.HIGHEST
high = lax.Precision.HIGH
f32 = jnp.float32
bf16 = jnp.bfloat16


def split(x):
    upper = x.astype(bf16)
    return upper, (x - upper.astype(f32)).astype(bf16)


def stack_right(x):
    upper, lower = split(x)
    return jnp.concatenate([upper, lower, upper], axis=0)


def stack_left(x):
    upper, lower = split(x)
    return jnp.concatenate([upper, lower, upper], axis=1)


def dot(a, b):
    return jnp.dot(a, b, preferred_element_type=f32)


def pair_kernel(ncol, place, own_ref, *refs):
    nown = own_ref.shape[0]
    far_refs = refs[:nown]
    (left_ref, left_own_ref, right_ref, hi_ref, hown_ref, hj_ref, ladder_ref, ladder_own_ref,
     pauli_ref, pauli_own_ref, out_ref, field, hcat, hown, wcat) = refs[nown:]
    orbs = ladder_ref.shape[0]
    half = orbs // 2
    _, _, _, nr, nc = own_ref.shape
    mine, me = place[0], place[1]

    @pl.when(pl.program_id(0) == 0)
    def _():
        upper, lower = split(hi_ref[...])
        hcat[...] = jnp.concatenate([upper, upper, lower], axis=1)
        upper, lower = split(hown_ref[...])
        hown[...] = jnp.concatenate([upper, upper, lower], axis=1)
        upper, lower = split(hj_ref[...])
        wcat[...] = jnp.concatenate([upper, upper, lower], axis=0)

    for n in range(nown):
        r, c = divmod(n, ncol)
        low = pl.multiple_of(mine * half + r * nr, nr)
        source = me ^ n
        far_low = pl.multiple_of((1 - mine) * half + lax.div(source, ncol) * nr, nr)
        far_col = pl.multiple_of(lax.rem(source, ncol) * nc, nc)
        for d in range(2):
            field[pl.ds(d * orbs + low, nr), pl.ds(c * nc, nc)] = own_ref[n, 0, d]
            field[pl.ds(d * orbs + far_low, nr), pl.ds(far_col, nc)] = far_refs[n][0, d]

    def apply(x, matrix, rhs, lhs, ladder):
        size = x.shape[0] // 2
        rows = dot(matrix, rhs)
        cols = dot(lhs, wcat[...])
        re = rows[:size] + (cols[:size, :orbs] - cols[size:, orbs:]) + ladder * x[:size]
        im = rows[size:] + (cols[:size, orbs:] + cols[size:, :orbs]) + ladder * x[size:]
        return re, im

    def source_of(left, pauli):
        lre, lim = left[0, 0], left[0, 1]
        rre, rim = right_ref[0, 0], right_ref[0, 1]
        return pauli * (lre * rre - lim * rim), pauli * (lre * rim + lim * rre)

    x = field[...]
    sre, sim = source_of(left_ref, pauli_ref[...])
    mre, mim = apply(x, hcat[...], stack_right(x), stack_left(x), ladder_ref[...])
    field[pl.ds(0, orbs), :] = mre + sre
    field[pl.ds(orbs, orbs), :] = mim + sim
    low = pl.multiple_of(mine * half, half)
    pre = field[pl.ds(low, half), :]
    pim = field[pl.ds(orbs + low, half), :]
    x = jnp.concatenate([pre, pim], axis=0)
    vre, vim = apply(x, hown[...], stack_right(field[...]), stack_left(x), ladder_own_ref[...])
    sre, sim = source_of(left_own_ref, pauli_own_ref[...])
    qre, qim = pre - 0.5 * sre, pim - 0.5 * sim
    scale = 0.5 * time_step * time_step
    ure = time_step * pim - scale * vre
    uim = -time_step * pre - scale * vim
    for n in range(nown):
        r, c = divmod(n, ncol)
        at = (slice(r * nr, (r + 1) * nr), slice(c * nc, (c + 1) * nc))
        out_ref[n, 0, 0] = qre[at]
        out_ref[n, 0, 1] = qim[at]
        out_ref[n, 0, 2] = ure[at]
        out_ref[n, 0, 3] = uim[at]


def pair_apply(ncol, place, own, far, left, left_own, right, constants):
    nown, nk, _, nr, nc = own.shape
    orbs = right.shape[-1]
    half = orbs // 2
    block = pl.BlockSpec((nown, 1, 2, nr, nc), lambda k, place: (0, k, 0, 0, 0))

    def each(a):
        return pl.BlockSpec((1,) + a.shape[1:], lambda k, place: (k, 0, 0, 0))

    def whole(a):
        return pl.BlockSpec(a.shape, lambda k, place: (0, 0))

    return pl.pallas_call(
        functools.partial(pair_kernel, ncol),
        grid_spec=pltpu.PrefetchScalarGridSpec(
            num_scalar_prefetch=1,
            grid=(nk,),
            in_specs=[block]
            + [each(a) for a in far]
            + [each(left), each(left_own), each(right)]
            + [whole(a) for a in constants],
            out_specs=pl.BlockSpec((nown, 1, 4, nr, nc), lambda k, place: (0, k, 0, 0, 0)),
            scratch_shapes=[
                pltpu.VMEM((2 * orbs, orbs), f32),
                pltpu.VMEM((2 * orbs, 6 * orbs), bf16),
                pltpu.VMEM((2 * half, 6 * orbs), bf16),
                pltpu.VMEM((3 * orbs, 2 * orbs), bf16),
            ],
        ),
        out_shape=jax.ShapeDtypeStruct((nown, nk, 4, nr, nc), f32),
        compiler_params=pltpu.CompilerParams(vmem_limit_bytes=48 * 1024 * 1024),
        cost_estimate=pl.CostEstimate(
            flops=nk * 72 * orbs**3, bytes_accessed=16 * own.size, transcendentals=0
        ),
    )(place, own, *far, left, left_own, right, *constants)


def on_device(nquad, ncol, chunks, green, hamiltonian, onebody, site_map, onsite_u, pair_first, pair_second):
    orbs, nr, nc = green.shape[1:]
    nown = nquad * ncol
    half = orbs // 2
    nk = orbs // (nown * chunks)
    mine = lax.axis_index("half")
    me = lax.axis_index("quad") * ncol + lax.axis_index("col")
    place = jnp.stack([mine, me]).astype(jnp.int32)

    packed = jnp.transpose(green.reshape(2, nown, chunks, nk, nr, nc), (2, 1, 3, 0, 4, 5))

    def exchange(x):
        return lax.all_to_all(x, ("quad", "col"), split_axis=0, concat_axis=0, tiled=True)

    def across(x, m):
        part = lax.dynamic_index_in_dim(x, me ^ m, 0, keepdims=False)
        pairs = [(s * nown + e, (1 - s) * nown + (e ^ m)) for s in range(2) for e in range(nown)]
        return lax.ppermute(part, ("half", "quad", "col"), pairs)

    far = [[across(packed[n], m) for m in range(nown)] for n in range(chunks)]
    own = [exchange(packed[n]) for n in range(chunks)]

    levels = jnp.arange(onsite_u.shape[0], dtype=jnp.int32)
    u_rows = jnp.sum(jnp.where(site_map[:, None] == levels[None, :], onsite_u[None, :], 0.0), axis=1)
    ladder = u_rows[:, None] * (site_map[:, None] == site_map[None, :]).astype(f32)
    orbitals = jnp.arange(orbs, dtype=jnp.int32)
    first_hot = (orbitals[:, None] == pair_first[None, :]).astype(bf16)
    second_hot = (orbitals[:, None] == pair_second[None, :]).astype(bf16)
    counts = jnp.einsum("ip,jp->ij", first_hot, second_hot, preferred_element_type=f32)
    pauli = u_rows[:, None] * counts

    hre, him = hamiltonian[0], hamiltonian[1]
    hi = jnp.concatenate(
        [jnp.concatenate([hre, -him], axis=1), jnp.concatenate([him, hre], axis=1)], axis=0
    )
    hj = jnp.concatenate([hre.T, him.T], axis=1)
    square = jnp.dot(hi, hi, precision=highest)
    spin = jnp.concatenate([hi[orbs:], -hi[:orbs]], axis=0)
    scale = 0.5 * time_step * time_step
    near = (time_step * spin - scale * square).reshape(2, orbs, 2, orbs)
    cross = (-2.0 * scale * hi).reshape(2, orbs, 2, nown, chunks, nk)

    def rows_of(a, axis):
        return lax.dynamic_slice_in_dim(a, mine * half, half, axis)

    hown = rows_of(hi.reshape(2, orbs, 2 * orbs), 1).reshape(2 * half, 2 * orbs)
    constants = (hi, hown, hj, ladder, rows_of(ladder, 0), pauli, rows_of(pauli, 0))
    body = lax.dynamic_slice_in_dim(onebody, me * (chunks * nk), chunks * nk, 1)
    body = jnp.transpose(body.reshape(2, chunks, nk, orbs), (1, 2, 0, 3))
    body_own = rows_of(body, 3)

    fields, ends = [], []
    for n in range(chunks):
        both = pair_apply(
            ncol, place, own[n], far[n], body[n][..., None], body_own[n][..., None],
            body[n][:, :, None, :], constants,
        )
        both = exchange(both)
        fields.append(both[:, :, :2])
        ends.append(both[:, :, 2:])
    total = lax.optimization_barrier(
        green + jnp.einsum("ckdl,dlij->ckij", near, green, precision=high)
    )
    for n in range(chunks):
        total = lax.optimization_barrier(
            total + jnp.einsum("ckdxt,xtdij->ckij", cross[:, :, :, :, n], fields[n], precision=high)
        )
    rest = jnp.stack([jnp.transpose(e, (2, 0, 1, 3, 4)) for e in ends], axis=2)
    return total + rest.reshape(green.shape)


def solution(mesh):
    nrow, ncol = mesh.shape["row"], mesh.shape["col"]
    halves = Mesh(
        mesh.devices.reshape(mesh.shape["grp"], 2, nrow // 2, ncol),
        ("grp", "half", "quad", "col"),
    )
    field = P("grp", None, ("half", "quad"), "col")
    placed = (field, P("grp", None, None), P("grp", None, None), P(), P(), P(), P())
    return jax.shard_map(
        functools.partial(on_device, nrow // 2, ncol, 4),
        mesh=halves,
        in_specs=placed,
        out_specs=field,
        check_vma=False,
    )
```

time: 1000 us -> 786 us (0.79)
  waiting for transfers between devices: 487 us -> 259 us
  starting transfers between devices: 37.5 us -> 151 us
  local copies, waits for them, and re-layouts: 216 us -> 111 us
  matrix products: 155 us -> 53.6 us
  Pallas kernels: 0 us -> 92.7 us
  blocking collectives: 23.6 us -> 89.9 us
  other arithmetic: 71.4 us -> 19.6 us
    all_to_all x6 -> x5, waiting for transfers between devices: 487 us -> 3.08 us  [exchange(): lax.all_to_all(x, ('quad', 'col'), split_axis=0, concat_axis=0, tiled=True)]
    ppermute x0 -> x32, waiting for transfers between devices: none -> 256 us  [across(): return lax.ppermute(part, ('half', 'quad', 'col'), pairs)]
    dot_general x25 -> x7, matrix products: 155 us -> 53.6 us  [the longest x1 29.2 us: on_device(): jnp.einsum('ckdl,dlij->ckij', near, green, precision=high)]
    pallas_call x0 -> x4, Pallas kernels: none -> 92.7 us  [pair_apply(): pl.pallas_call(functools.partial(pair_kernel, ncol), grid_spec=pltpu.Pref...]
    all_to_all x8 -> x0, local copies, waits for them, and re-layouts: 88.1 us -> none  [the longest x2 30.8 us: force(): lax.all_to_all(field, 'col', split_axis=1, concat_axis=3, tiled=True)]
    ppermute x0 -> x32, starting transfers between devices: none -> 77.7 us  [across(): return lax.ppermute(part, ('half', 'quad', 'col'), pairs)]
    all_to_all x2 -> x3, blocking collectives: 23.6 us -> 89.9 us  [exchange(): lax.all_to_all(x, ('quad', 'col'), split_axis=0, concat_axis=0, tiled=True)]
    add x8 -> x1, other arithmetic: 55.8 us -> 14.1 us  [on_device(): return total + rest.reshape(green.shape)]
  transfers between devices with their start and end apart: 6 -> 37, of which waited for: 4 -> 30; matrix products, arithmetic and copies ran while one was open for 35% -> 10% of each run, Pallas kernels for 0% -> 12%
where the time goes in v1:
time: 786 us; the launch traced here: 777 us
  waiting for transfers between devices  259 us (33%)
  starting transfers between devices  151 us (19%)
  local copies, waits for them, and re-layouts  111 us (14%)
  Pallas kernels  92.7 us (12%)
  blocking collectives  89.9 us (11%)
  matrix products  53.6 us (7%)
  other arithmetic  19.6 us (2%)
    ppermute x32, waiting for transfers between devices, across(): return lax.ppermute(part, ('half', 'quad', 'col'), pairs)  256 us
    pallas_call x4, Pallas kernels, pair_apply(): pl.pallas_call(functools.partial(pair_kernel, ncol), grid_spec=pltpu.Pref...  92.7 us
    all_to_all x3, blocking collectives, exchange(): lax.all_to_all(x, ('quad', 'col'), split_axis=0, concat_axis=0, tiled=True)  89.9 us
    ppermute x32, starting transfers between devices, across(): return lax.ppermute(part, ('half', 'quad', 'col'), pairs)  77.7 us
    all_to_all x5, starting transfers between devices, exchange(): lax.all_to_all(x, ('quad', 'col'), split_axis=0, concat_axis=0, tiled=True)  72.9 us
    unnamed x122, local copies, waits for them, and re-layouts  29.4 us
    dot_general x1, matrix products, on_device(): jnp.einsum('ckdl,dlij->ckij', near, green, precision=high)  29.2 us
    another operation x5, local copies, waits for them, and re-layouts, on_device(): rest = jnp.stack([jnp.transpose(e, (2, 0, 1, 3, 4)) for e in ends], axis=2)  23.4 us
  transfers between devices with their start and end apart: 37, of which 30 were waited for; matrix products, arithmetic and copies ran while one was open for 10% of the time, Pallas kernels for 12%

profile of v1, /device:TPU:0, one launch (start us, length us, event | category | flops | bytes accessed | tf_op | source)
XLA Modules:
  0.0 776.8 jit_solution(4089295695132887622)
XLA Ops:
  0.0 8.3 %copy.289 = f32[2,8,4,8,32,128]{5,4,0,3,1,2:T(8,128)} copy(f32[2,8,4,8,32,128]{5,4,3,2,1,0:T(8,128)} %bitcast.204) | data formatting | bytes 16777216 | tf_op jit(solution)/shard_map/reshape | solution.py:148
  8.3 8.6 %fusion.19 = (f32[1,8,8,2,32,128]{5,4,3,2,1,0:T(8,128)S(1)}, f32[8,8,2,32,128]{4,3,2,1,0:T(8,128)}, f32[8,8,2,32,128]{4,3,2,1,0:T(8,128)S(1)}, f32[8,8,2,32,128]...) fusion(f32[4,8,8,2,32,128]{5,4,3,2,1,0:T(8,128)} %bitcast.206), kind=kLoop, calls=%fused_computation.100 | loop fusion | bytes 25165824 | tf_op jit(solution)/shard_map/slice | solution.py:159
  16.9 31.5 %all_to_all.40.own_ref = f32[8,8,2,32,128]{4,3,2,1,0:T(8,128)} all-to-all(f32[8,8,2,32,128]{4,3,2,1,0:T(8,128)} %get-tuple-element.9), channel_id=1, replica_groups=mesh['grp'=2,'half'=2,'quad'=4,'col'=2] {'quad','col'}, dimensions={0} | all-to-all | bytes 4194304 | tf_op jit(solution)/shard_map/all_to_all | solution.py:151
  48.5 29.2 %all_to_all.41.own_ref = f32[8,8,2,32,128]{4,3,2,1,0:T(8,128)} all-to-all(f32[8,8,2,32,128]{4,3,2,1,0:T(8,128)S(1)} %copy-done.42), channel_id=1, replica_groups=mesh['grp'=2,'half'=2,'quad'=4,'col'=2] {'quad','col'}, dimensions={0} | all-to-all | bytes 4194304 | tf_op jit(solution)/shard_map/all_to_all | solution.py:151
  77.6 29.2 %all_to_all.42.own_ref = f32[8,8,2,32,128]{4,3,2,1,0:T(8,128)} all-to-all(f32[8,8,2,32,128]{4,3,2,1,0:T(8,128)S(1)} %get-tuple-element.7), channel_id=1, replica_groups=mesh['grp'=2,'half'=2,'quad'=4,'col'=2] {'quad','col'}, dimensions={0} | all-to-all | bytes 4194304 | tf_op jit(solution)/shard_map/all_to_all | solution.py:151
  131.8 8.9 %collective-permute-done.24.refs_0_ = f32[8,2,32,128]{3,2,1,0:T(8,128)S(1)} collective-permute-done((f32[8,2,32,128]{3,2,1,0:T(8,128)}, f32[8,2,32,128]{3,2,1,0:T(8,128)S(1)}, u32[]{:S(2)}, u32[]{:S(2)}) %collective-permute-start.24) | collective-permute-done | bytes 262176 | tf_op jit(solution)/shard_map/ppermute | solution.py:156
  146.3 5.2 collective-permute-start.30
  161.6 6.3 collective-permute-done.28.refs_4_
  172.6 7.5 collective-permute-done.30.refs_6_
  189.9 23.1 %shard_map.76 = f32[8,8,4,32,128]{4,3,2,1,0:T(8,128)} custom-call(s32[2]{0:T(128)S(1)} %copy-done.38, f32[8,8,2,32,128]{4,3,2,1,0:T(8,128)} %all_to_all.40.own_ref, f32[8,2,32,128]{3,2,1,0:T(8,128)S(1)} %copy-done.15, f32[8,2,32,128]{3,2,1,0:T(8,128)S(1)} %copy-done.17, f32[8,2,32,128]{3,2,1,0:T(8,128)S(1)} %copy-done.19, ...), custom_call_target="tpu_custom_call" | custom-call | flops 9663676416 | bytes 8388608 | tf_op jit(solution)/shard_map/pallas_call | solution.py:114
  213.1 25.6 %all-to-all-start.7 = ((f32[8,8,4,32,128]{4,3,2,1,0:T(8,128)}), f32[8,8,4,32,128]{4,3,2,1,0:T(8,128)}, u32[]{:S(2)}, u32[]{:S(2)}) async-start(f32[8,8,4,32,128]{4,3,2,1,0:T(8,128)} %shard_map.76), calls=%async_computation.7 | async-start | bytes 8388608 | tf_op jit(solution)/shard_map/all_to_all | solution.py:151
  253.3 37.2 %collective-permute-done.16.refs_0_ = f32[8,2,32,128]{3,2,1,0:T(8,128)S(1)} collective-permute-done((f32[8,2,32,128]{3,2,1,0:T(8,128)S(1)}, f32[8,2,32,128]{3,2,1,0:T(8,128)S(1)}, u32[]{:S(2)}, u32[]{:S(2)}) %collective-permute-start.16) | collective-permute-done | bytes 262176 | tf_op jit(solution)/shard_map/ppermute | solution.py:156
  296.8 6.6 collective-permute-start.22
  311.7 7.6 collective-permute-done.20.refs_4_
  324.0 7.5 collective-permute-done.22.refs_6_
  342.2 23.2 %shard_map.75 = f32[8,8,4,32,128]{4,3,2,1,0:T(8,128)} custom-call(s32[2]{0:T(128)S(1)} %copy-done.39, f32[8,8,2,32,128]{4,3,2,1,0:T(8,128)} %all_to_all.41.own_ref, f32[8,2,32,128]{3,2,1,0:T(8,128)S(1)} %copy-done.27, f32[8,2,32,128]{3,2,1,0:T(8,128)S(1)} %copy-done.31, f32[8,2,32,128]{3,2,1,0:T(8,128)S(1)} %copy-done.35, ...), custom_call_target="tpu_custom_call" | custom-call | flops 9663676416 | bytes 8388608 | tf_op jit(solution)/shard_map/pallas_call | solution.py:114
  365.4 19.1 %all-to-all-start.5 = ((f32[8,8,4,32,128]{4,3,2,1,0:T(8,128)}), f32[8,8,4,32,128]{4,3,2,1,0:T(8,128)}, u32[]{:S(2)}, u32[]{:S(2)}) async-start(f32[8,8,4,32,128]{4,3,2,1,0:T(8,128)} %shard_map.75), calls=%async_computation.5 | async-start | bytes 8388608 | tf_op jit(solution)/shard_map/all_to_all | solution.py:151
  397.7 38.6 %collective-permute-done.10.refs_2_ = f32[8,2,32,128]{3,2,1,0:T(8,128)S(1)} collective-permute-done((f32[8,2,32,128]{3,2,1,0:T(8,128)S(1)}, f32[8,2,32,128]{3,2,1,0:T(8,128)S(1)}, u32[]{:S(2)}, u32[]{:S(2)}) %collective-permute-start.10) | collective-permute-done | bytes 262176 | tf_op jit(solution)/shard_map/ppermute | solution.py:156
  455.6 7.4 collective-permute-done.14.refs_6_
  467.7 21.9 %collective-permute-done.8.refs_0_ = f32[8,2,32,128]{3,2,1,0:T(8,128)} collective-permute-done((f32[8,2,32,128]{3,2,1,0:T(8,128)}, f32[8,2,32,128]{3,2,1,0:T(8,128)}, u32[]{:S(2)}, u32[]{:S(2)}) %collective-permute-start.8) | collective-permute-done | bytes 262176 | tf_op jit(solution)/shard_map/ppermute | solution.py:156
  489.5 5.7 collective-permute-done.9.refs_1_
  501.3 23.2 %shard_map.74 = f32[8,8,4,32,128]{4,3,2,1,0:T(8,128)} custom-call(s32[2]{0:T(128)S(1)} %copy-done.40, f32[8,8,2,32,128]{4,3,2,1,0:T(8,128)} %all_to_all.42.own_ref, f32[8,2,32,128]{3,2,1,0:T(8,128)} %collective-permute-done.8.refs_0_, f32[8,2,32,128]{3,2,1,0:T(8,128)} %collective-permute-done.9.refs_1_, f32[8,2,32,128]{3,2,1,0:T(8,128)S(1)} %copy-done.29, ...), custom_call_target="tpu_custom_call" | custom-call | flops 9663676416 | bytes 8388608 | tf_op jit(solution)/shard_map/pallas_call | solution.py:114
  539.5 41.3 %collective-permute-done.refs_0_ = f32[8,2,32,128]{3,2,1,0:T(8,128)S(1)} collective-permute-done((f32[8,2,32,128]{3,2,1,0:T(8,128)S(1)}, f32[8,2,32,128]{3,2,1,0:T(8,128)S(1)}, u32[]{:S(2)}, u32[]{:S(2)}) %collective-permute-start) | collective-permute-done | bytes 262176 | tf_op jit(solution)/shard_map/ppermute | solution.py:156
  597.9 7.6 collective-permute-done.4.refs_4_
  610.1 7.7 collective-permute-done.6.refs_6_
  627.6 23.2 %shard_map.73 = f32[8,8,4,32,128]{4,3,2,1,0:T(8,128)} custom-call(s32[2]{0:T(128)S(1)} %copy-done.41, f32[8,8,2,32,128]{4,3,2,1,0:T(8,128)} %all-to-all-done.own_ref, f32[8,2,32,128]{3,2,1,0:T(8,128)S(1)} %copy-done.21, f32[8,2,32,128]{3,2,1,0:T(8,128)S(1)} %copy-done.23, f32[8,2,32,128]{3,2,1,0:T(8,128)S(1)} %copy-done.25, ...), custom_call_target="tpu_custom_call" | custom-call | flops 9663676416 | bytes 8388608 | tf_op jit(solution)/shard_map/pallas_call | solution.py:114
  650.9 19.2 %all-to-all-start.1 = ((f32[8,8,4,32,128]{4,3,2,1,0:T(8,128)}), f32[8,8,4,32,128]{4,3,2,1,0:T(8,128)}, u32[]{:S(2)}, u32[]{:S(2)}) async-start(f32[8,8,4,32,128]{4,3,2,1,0:T(8,128)} %shard_map.73), calls=%async_computation.1 | async-start | bytes 8388608 | tf_op jit(solution)/shard_map/all_to_all | solution.py:151
  672.8 29.2 %bitcast_add_fusion.4 = f32[2,256,32,128]{3,1,2,0:T(8,128)} fusion(f32[2,256,32,128]{3,2,1,0:T(8,128)} %param.7, f32[2,256,2,256,1]{1,0,3,2,4:T(2,128)S(1)} %bitcast.209), kind=kOutput, calls=%fused_computation.5 | convolution fusion | flops 6444548096 | bytes 17825792 | tf_op jit(solution)/shard_map/ckdl,dlij->ckij/dot_general | solution.py:200
  706.3 5.1 slice_bitcast_fusion.1
  743.3 7.4 bitcast_add_fusion
  750.7 14.1 %copy_add_fusion = f32[2,256,32,128]{3,1,2,0:T(8,128)} fusion(f32[2,256,32,128]{3,1,2,0:T(8,128)} %bitcast_add_fusion, f32[2,256,32,128]{3,2,1,0:T(8,128)} %bitcast.205), kind=kLoop, calls=%fused_computation.8 | loop fusion | flops 2097152 | bytes 25165824 | tf_op jit(solution)/shard_map/add | solution.py:207
  764.8 11.7 %copy.233 = f32[2,256,32,128]{3,2,1,0:T(8,128)} copy(f32[2,256,32,128]{3,1,2,0:T(8,128)} %copy_add_fusion) | data formatting | bytes 16777216 | tf_op jit(solution)/shard_map/add | solution.py:207
  (221 shorter events, 227.9 us)
Async XLA Ops:
  106.8 106.3 %all-to-all-start = ((f32[8,8,2,32,128]{4,3,2,1,0:T(8,128)}), f32[8,8,2,32,128]{4,3,2,1,0:T(8,128)}, u32[]{:S(2)}, u32[]{:S(2)}) async-start(f32[8,8,2,32,128]{4,3,2,1,0:T(8,128)} %get-tuple-element.6), calls=%async_computation | async-start | bytes 4194304 | tf_op jit(solution)/shard_map/all_to_all | solution.py:151
  115.5 30.7 %collective-permute-start.25 = (f32[8,2,32,128]{3,2,1,0:T(8,128)}, f32[8,2,32,128]{3,2,1,0:T(8,128)S(1)}, u32[]{:S(2)}, u32[]{:S(2)}) collective-permute-start(f32[8,2,32,128]{3,2,1,0:T(8,128)} %get-tuple-element.27), channel_id=1, source_target_pairs={{0,9},{1,8},{2,11},{3,10},{4,13},{5,12},{6,15},{7,14},{8,1},{9,0},... | collective-permute-start | bytes 786440 | tf_op jit(solution)/shard_map/ppermute | solution.py:156
  115.5 36.3 %collective-permute-start.26 = (f32[8,2,32,128]{3,2,1,0:T(8,128)}, f32[8,2,32,128]{3,2,1,0:T(8,128)S(1)}, u32[]{:S(2)}, u32[]{:S(2)}) collective-permute-start(f32[8,2,32,128]{3,2,1,0:T(8,128)} %get-tuple-element.26), channel_id=1, source_target_pairs={{0,10},{1,11},{2,8},{3,9},{4,14},{5,15},{6,12},{7,13},{8,2},{9,3},... | collective-permute-start | bytes 786440 | tf_op jit(solution)/shard_map/ppermute | solution.py:156
  119.2 42.4 %collective-permute-start.27 = (f32[8,2,32,128]{3,2,1,0:T(8,128)}, f32[8,2,32,128]{3,2,1,0:T(8,128)}, u32[]{:S(2)}, u32[]{:S(2)}) collective-permute-start(f32[8,2,32,128]{3,2,1,0:T(8,128)} %get-tuple-element.25), channel_id=1, source_target_pairs={{0,11},{1,10},{2,9},{3,8},{4,15},{5,14},{6,13},{7,12},{8,3},{9,2},... | collective-permute-start | bytes 786440 | tf_op jit(solution)/shard_map/ppermute | solution.py:156
  119.5 48.4 %collective-permute-start.28 = (f32[8,2,32,128]{3,2,1,0:T(8,128)}, f32[8,2,32,128]{3,2,1,0:T(8,128)}, u32[]{:S(2)}, u32[]{:S(2)}) collective-permute-start(f32[8,2,32,128]{3,2,1,0:T(8,128)} %get-tuple-element.24), channel_id=1, source_target_pairs={{0,12},{1,13},{2,14},{3,15},{4,8},{5,9},{6,10},{7,11},{8,4},{9,5},... | collective-permute-start | bytes 786440 | tf_op jit(solution)/shard_map/ppermute | solution.py:156
  140.7 31.9 %collective-permute-start.29 = (f32[8,2,32,128]{3,2,1,0:T(8,128)}, f32[8,2,32,128]{3,2,1,0:T(8,128)}, u32[]{:S(2)}, u32[]{:S(2)}) collective-permute-start(f32[8,2,32,128]{3,2,1,0:T(8,128)} %get-tuple-element.23), channel_id=1, source_target_pairs={{0,13},{1,12},{2,15},{3,14},{4,9},{5,8},{6,11},{7,10},{8,5},{9,4},... | collective-permute-start | bytes 786440 | tf_op jit(solution)/shard_map/ppermute | solution.py:156
  146.3 33.8 %collective-permute-start.30 = (f32[8,2,32,128]{3,2,1,0:T(8,128)}, f32[8,2,32,128]{3,2,1,0:T(8,128)}, u32[]{:S(2)}, u32[]{:S(2)}) collective-permute-start(f32[8,2,32,128]{3,2,1,0:T(8,128)} %get-tuple-element.22), channel_id=1, source_target_pairs={{0,14},{1,15},{2,12},{3,13},{4,10},{5,11},{6,8},{7,9},{8,6},{9,7},... | collective-permute-start | bytes 786440 | tf_op jit(solution)/shard_map/ppermute | solution.py:156
  151.9 32.9 %collective-permute-start.31 = (f32[8,2,32,128]{3,2,1,0:T(8,128)}, f32[8,2,32,128]{3,2,1,0:T(8,128)}, u32[]{:S(2)}, u32[]{:S(2)}) collective-permute-start(f32[8,2,32,128]{3,2,1,0:T(8,128)} %get-tuple-element.21), channel_id=1, source_target_pairs={{0,15},{1,14},{2,13},{3,12},{4,11},{5,10},{6,9},{7,8},{8,7},{9,6},... | collective-permute-start | bytes 786440 | tf_op jit(solution)/shard_map/ppermute | solution.py:156
  213.1 152.3 %all-to-all-start.7 = ((f32[8,8,4,32,128]{4,3,2,1,0:T(8,128)}), f32[8,8,4,32,128]{4,3,2,1,0:T(8,128)}, u32[]{:S(2)}, u32[]{:S(2)}) async-start(f32[8,8,4,32,128]{4,3,2,1,0:T(8,128)} %shard_map.76), calls=%async_computation.7 | async-start | bytes 8388608 | tf_op jit(solution)/shard_map/all_to_all | solution.py:151
  241.4 49.2 %collective-permute-start.16 = (f32[8,2,32,128]{3,2,1,0:T(8,128)S(1)}, f32[8,2,32,128]{3,2,1,0:T(8,128)S(1)}, u32[]{:S(2)}, u32[]{:S(2)}) collective-permute-start(f32[8,2,32,128]{3,2,1,0:T(8,128)S(1)} %get-tuple-element.36), channel_id=1, source_target_pairs={{0,8},{1,9},{2,10},{3,11},{4,12},{5,13},{6,14},{7,15},{8,0},{9,1},... | collective-permute-start | bytes 786440 | tf_op jit(solution)/shard_map/ppermute | solution.py:156
  245.7 50.4 %collective-permute-start.17 = (f32[8,2,32,128]{3,2,1,0:T(8,128)S(1)}, f32[8,2,32,128]{3,2,1,0:T(8,128)S(1)}, u32[]{:S(2)}, u32[]{:S(2)}) collective-permute-start(f32[8,2,32,128]{3,2,1,0:T(8,128)S(1)} %get-tuple-element.35), channel_id=1, source_target_pairs={{0,9},{1,8},{2,11},{3,10},{4,13},{5,12},{6,15},{7,14},{8,1},{9,0},... | collective-permute-start | bytes 786440 | tf_op jit(solution)/shard_map/ppermute | solution.py:156
  245.9 57.6 %collective-permute-start.18 = (f32[8,2,32,128]{3,2,1,0:T(8,128)S(1)}, f32[8,2,32,128]{3,2,1,0:T(8,128)S(1)}, u32[]{:S(2)}, u32[]{:S(2)}) collective-permute-start(f32[8,2,32,128]{3,2,1,0:T(8,128)S(1)} %get-tuple-element.34), channel_id=1, source_target_pairs={{0,10},{1,11},{2,8},{3,9},{4,14},{5,15},{6,12},{7,13},{8,2},{9,3},... | collective-permute-start | bytes 786440 | tf_op jit(solution)/shard_map/ppermute | solution.py:156
  249.5 62.2 %collective-permute-start.19 = (f32[8,2,32,128]{3,2,1,0:T(8,128)}, f32[8,2,32,128]{3,2,1,0:T(8,128)}, u32[]{:S(2)}, u32[]{:S(2)}) collective-permute-start(f32[8,2,32,128]{3,2,1,0:T(8,128)} %get-tuple-element.33), channel_id=1, source_target_pairs={{0,11},{1,10},{2,9},{3,8},{4,15},{5,14},{6,13},{7,12},{8,3},{9,2},... | collective-permute-start | bytes 786440 | tf_op jit(solution)/shard_map/ppermute | solution.py:156
  249.8 69.5 %collective-permute-start.20 = (f32[8,2,32,128]{3,2,1,0:T(8,128)}, f32[8,2,32,128]{3,2,1,0:T(8,128)}, u32[]{:S(2)}, u32[]{:S(2)}) collective-permute-start(f32[8,2,32,128]{3,2,1,0:T(8,128)} %get-tuple-element.32), channel_id=1, source_target_pairs={{0,12},{1,13},{2,14},{3,15},{4,8},{5,9},{6,10},{7,11},{8,4},{9,5},... | collective-permute-start | bytes 786440 | tf_op jit(solution)/shard_map/ppermute | solution.py:156
  291.2 32.8 %collective-permute-start.21 = (f32[8,2,32,128]{3,2,1,0:T(8,128)}, f32[8,2,32,128]{3,2,1,0:T(8,128)}, u32[]{:S(2)}, u32[]{:S(2)}) collective-permute-start(f32[8,2,32,128]{3,2,1,0:T(8,128)} %get-tuple-element.31), channel_id=1, source_target_pairs={{0,13},{1,12},{2,15},{3,14},{4,9},{5,8},{6,11},{7,10},{8,5},{9,4},... | collective-permute-start | bytes 786440 | tf_op jit(solution)/shard_map/ppermute | solution.py:156
  296.8 34.6 %collective-permute-start.22 = (f32[8,2,32,128]{3,2,1,0:T(8,128)}, f32[8,2,32,128]{3,2,1,0:T(8,128)}, u32[]{:S(2)}, u32[]{:S(2)}) collective-permute-start(f32[8,2,32,128]{3,2,1,0:T(8,128)} %get-tuple-element.30), channel_id=1, source_target_pairs={{0,14},{1,15},{2,12},{3,13},{4,10},{5,11},{6,8},{7,9},{8,6},{9,7},... | collective-permute-start | bytes 786440 | tf_op jit(solution)/shard_map/ppermute | solution.py:156
  304.2 32.0 %collective-permute-start.23 = (f32[8,2,32,128]{3,2,1,0:T(8,128)}, f32[8,2,32,128]{3,2,1,0:T(8,128)}, u32[]{:S(2)}, u32[]{:S(2)}) collective-permute-start(f32[8,2,32,128]{3,2,1,0:T(8,128)} %get-tuple-element.29), channel_id=1, source_target_pairs={{0,15},{1,14},{2,13},{3,12},{4,11},{5,10},{6,9},{7,8},{8,7},{9,6},... | collective-permute-start | bytes 786440 | tf_op jit(solution)/shard_map/ppermute | solution.py:156
  365.4 159.1 %all-to-all-start.5 = ((f32[8,8,4,32,128]{4,3,2,1,0:T(8,128)}), f32[8,8,4,32,128]{4,3,2,1,0:T(8,128)}, u32[]{:S(2)}, u32[]{:S(2)}) async-start(f32[8,8,4,32,128]{4,3,2,1,0:T(8,128)} %shard_map.75), calls=%async_computation.5 | async-start | bytes 8388608 | tf_op jit(solution)/shard_map/all_to_all | solution.py:151
  387.1 49.3 %collective-permute-start.10 = (f32[8,2,32,128]{3,2,1,0:T(8,128)S(1)}, f32[8,2,32,128]{3,2,1,0:T(8,128)S(1)}, u32[]{:S(2)}, u32[]{:S(2)}) collective-permute-start(f32[8,2,32,128]{3,2,1,0:T(8,128)S(1)} %get-tuple-element.42), channel_id=1, source_target_pairs={{0,10},{1,11},{2,8},{3,9},{4,14},{5,15},{6,12},{7,13},{8,2},{9,3},... | collective-permute-start | bytes 786440 | tf_op jit(solution)/shard_map/ppermute | solution.py:156
  389.7 52.3 %collective-permute-start.11 = (f32[8,2,32,128]{3,2,1,0:T(8,128)S(1)}, f32[8,2,32,128]{3,2,1,0:T(8,128)S(1)}, u32[]{:S(2)}, u32[]{:S(2)}) collective-permute-start(f32[8,2,32,128]{3,2,1,0:T(8,128)S(1)} %get-tuple-element.41), channel_id=1, source_target_pairs={{0,11},{1,10},{2,9},{3,8},{4,15},{5,14},{6,13},{7,12},{8,3},{9,2},... | collective-permute-start | bytes 786440 | tf_op jit(solution)/shard_map/ppermute | solution.py:156
  390.7 60.1 %collective-permute-start.12 = (f32[8,2,32,128]{3,2,1,0:T(8,128)S(1)}, f32[8,2,32,128]{3,2,1,0:T(8,128)S(1)}, u32[]{:S(2)}, u32[]{:S(2)}) collective-permute-start(f32[8,2,32,128]{3,2,1,0:T(8,128)S(1)} %get-tuple-element.40), channel_id=1, source_target_pairs={{0,12},{1,13},{2,14},{3,15},{4,8},{5,9},{6,10},{7,11},{8,4},{9,5},... | collective-permute-start | bytes 786440 | tf_op jit(solution)/shard_map/ppermute | solution.py:156
  393.0 62.6 %collective-permute-start.13 = (f32[8,2,32,128]{3,2,1,0:T(8,128)}, f32[8,2,32,128]{3,2,1,0:T(8,128)}, u32[]{:S(2)}, u32[]{:S(2)}) collective-permute-start(f32[8,2,32,128]{3,2,1,0:T(8,128)} %get-tuple-element.39), channel_id=1, source_target_pairs={{0,13},{1,12},{2,15},{3,14},{4,9},{5,8},{6,11},{7,10},{8,5},{9,4},... | collective-permute-start | bytes 786440 | tf_op jit(solution)/shard_map/ppermute | solution.py:156
  394.2 68.8 %collective-permute-start.14 = (f32[8,2,32,128]{3,2,1,0:T(8,128)}, f32[8,2,32,128]{3,2,1,0:T(8,128)}, u32[]{:S(2)}, u32[]{:S(2)}) collective-permute-start(f32[8,2,32,128]{3,2,1,0:T(8,128)} %get-tuple-element.38), channel_id=1, source_target_pairs={{0,14},{1,15},{2,12},{3,13},{4,10},{5,11},{6,8},{7,9},{8,6},{9,7},... | collective-permute-start | bytes 786440 | tf_op jit(solution)/shard_map/ppermute | solution.py:156
  442.7 46.9 %collective-permute-start.8 = (f32[8,2,32,128]{3,2,1,0:T(8,128)}, f32[8,2,32,128]{3,2,1,0:T(8,128)}, u32[]{:S(2)}, u32[]{:S(2)}) collective-permute-start(f32[8,2,32,128]{3,2,1,0:T(8,128)} %get-tuple-element.44), channel_id=1, source_target_pairs={{0,8},{1,9},{2,10},{3,11},{4,12},{5,13},{6,14},{7,15},{8,0},{9,1},... | collective-permute-start | bytes 786440 | tf_op jit(solution)/shard_map/ppermute | solution.py:156
  451.6 43.7 %collective-permute-start.9 = (f32[8,2,32,128]{3,2,1,0:T(8,128)}, f32[8,2,32,128]{3,2,1,0:T(8,128)}, u32[]{:S(2)}, u32[]{:S(2)}) collective-permute-start(f32[8,2,32,128]{3,2,1,0:T(8,128)} %get-tuple-element.43), channel_id=1, source_target_pairs={{0,9},{1,8},{2,11},{3,10},{4,13},{5,12},{6,15},{7,14},{8,1},{9,0},... | collective-permute-start | bytes 786440 | tf_op jit(solution)/shard_map/ppermute | solution.py:156
  524.5 126.4 %all-to-all-start.3 = ((f32[8,8,4,32,128]{4,3,2,1,0:T(8,128)}), f32[8,8,4,32,128]{4,3,2,1,0:T(8,128)}, u32[]{:S(2)}, u32[]{:S(2)}) async-start(f32[8,8,4,32,128]{4,3,2,1,0:T(8,128)} %shard_map.74), calls=%async_computation.3 | async-start | bytes 8388608 | tf_op jit(solution)/shard_map/all_to_all | solution.py:151
  531.7 49.2 %collective-permute-start = (f32[8,2,32,128]{3,2,1,0:T(8,128)S(1)}, f32[8,2,32,128]{3,2,1,0:T(8,128)S(1)}, u32[]{:S(2)}, u32[]{:S(2)}) collective-permute-start(f32[8,2,32,128]{3,2,1,0:T(8,128)S(1)} %get-tuple-element.52), channel_id=1, source_target_pairs={{0,8},{1,9},{2,10},{3,11},{4,12},{5,13},{6,14},{7,15},{8,0},{9,1},... | collective-permute-start | bytes 786440 | tf_op jit(solution)/shard_map/ppermute | solution.py:156
  531.7 54.9 %collective-permute-start.1 = (f32[8,2,32,128]{3,2,1,0:T(8,128)S(1)}, f32[8,2,32,128]{3,2,1,0:T(8,128)S(1)}, u32[]{:S(2)}, u32[]{:S(2)}) collective-permute-start(f32[8,2,32,128]{3,2,1,0:T(8,128)S(1)} %get-tuple-element.51), channel_id=1, source_target_pairs={{0,9},{1,8},{2,11},{3,10},{4,13},{5,12},{6,15},{7,14},{8,1},{9,0},... | collective-permute-start | bytes 786440 | tf_op jit(solution)/shard_map/ppermute | solution.py:156
  534.3 57.9 %collective-permute-start.2 = (f32[8,2,32,128]{3,2,1,0:T(8,128)S(1)}, f32[8,2,32,128]{3,2,1,0:T(8,128)S(1)}, u32[]{:S(2)}, u32[]{:S(2)}) collective-permute-start(f32[8,2,32,128]{3,2,1,0:T(8,128)S(1)} %get-tuple-element.50), channel_id=1, source_target_pairs={{0,10},{1,11},{2,8},{3,9},{4,14},{5,15},{6,12},{7,13},{8,2},{9,3},... | collective-permute-start | bytes 786440 | tf_op jit(solution)/shard_map/ppermute | solution.py:156
  535.9 62.0 %collective-permute-start.3 = (f32[8,2,32,128]{3,2,1,0:T(8,128)}, f32[8,2,32,128]{3,2,1,0:T(8,128)}, u32[]{:S(2)}, u32[]{:S(2)}) collective-permute-start(f32[8,2,32,128]{3,2,1,0:T(8,128)} %get-tuple-element.49), channel_id=1, source_target_pairs={{0,11},{1,10},{2,9},{3,8},{4,15},{5,14},{6,13},{7,12},{8,3},{9,2},... | collective-permute-start | bytes 786440 | tf_op jit(solution)/shard_map/ppermute | solution.py:156
  537.9 67.6 %collective-permute-start.4 = (f32[8,2,32,128]{3,2,1,0:T(8,128)}, f32[8,2,32,128]{3,2,1,0:T(8,128)}, u32[]{:S(2)}, u32[]{:S(2)}) collective-permute-start(f32[8,2,32,128]{3,2,1,0:T(8,128)} %get-tuple-element.48), channel_id=1, source_target_pairs={{0,12},{1,13},{2,14},{3,15},{4,8},{5,9},{6,10},{7,11},{8,4},{9,5},... | collective-permute-start | bytes 786440 | tf_op jit(solution)/shard_map/ppermute | solution.py:156
  650.9 68.6 %all-to-all-start.1 = ((f32[8,8,4,32,128]{4,3,2,1,0:T(8,128)}), f32[8,8,4,32,128]{4,3,2,1,0:T(8,128)}, u32[]{:S(2)}, u32[]{:S(2)}) async-start(f32[8,8,4,32,128]{4,3,2,1,0:T(8,128)} %shard_map.73), calls=%async_computation.1 | async-start | bytes 8388608 | tf_op jit(solution)/shard_map/all_to_all | solution.py:151
  (65 other events, 564.4 us)
